TPU v7x, 32 devices: a whole 2x2x4 slice. The times are simulated.
32 devices in a mesh: inp: 8 (over z, x), tm: 4 (over y, core).
Axes of the slice: x: 2, y: 2, z: 4, core: 2. Of those that a mesh axis runs over, the one named last changes fastest.
Arguments:
- voltages: float32 [256, 256, 2048], P('inp', 'tm'), may hold values from -6 to 6
- filter_taps: float32 [4, 2048], replicated, may hold values from -1 to 2
Outputs:
- visibilities: float32 [2, 1024, 256, 256], P(None, ('inp', 'tm'))
All inputs are finite; a program needn't handle non-finite values.
Results may differ from a plain program's by a relative error of at most 0.000084.
Values sent between devices are 32-bit elements; how exact they have to be, the bound alone decides.
No kernel may reach another device: no remote copies, remote signals or barrier semaphores. Data moves between devices by JAX's collectives and lax.ppermute only.
A program may use at most 192 MiB of HBM per device.

v0:
```python
import math

import jax
import jax.numpy as jnp
from jax import lax
from jax.sharding import PartitionSpec as P


def from_behind(value, axis, steps):
    count = lax.axis_size(axis)
    leading, last = (max(0, -steps), min(count, count - steps))
    return lax.ppermute(value, axis, [(source, source + steps) for source in range(leading, last)])


def transform_table(nfft, half):
    channel = jnp.arange(half, dtype=jnp.int32)
    sample = jnp.arange(nfft, dtype=jnp.int32)
    phase = channel[:, None] * sample[None, :] % nfft
    angle = 2.0 * math.pi / nfft * phase.astype(jnp.float32)
    scale = 1.0 / math.sqrt(nfft)
    return jnp.concatenate([jnp.cos(angle), -jnp.sin(angle)], axis=0) * scale


def correlate_pair(rows, cols):
    return jnp.einsum("cas,cbs->cab", rows, cols, precision=lax.Precision.HIGHEST)


def on_device(voltages, filter_taps):
    inputs_dev = voltages.shape[0]
    frames_dev = voltages.shape[1]
    nfft = voltages.shape[2]
    taps = filter_taps.shape[0]
    half = nfft // 2
    history = from_behind(voltages[:, frames_dev - (taps - 1) :, :], "tm", 1)
    extended = jnp.concatenate([history, voltages], axis=1)
    filtered = filter_taps[0] * extended[:, 0:frames_dev, :]
    for k in range(1, taps):
        filtered = filtered + filter_taps[k] * extended[:, k : k + frames_dev, :]
    table = transform_table(nfft, half)
    spectra = jnp.einsum("kn,ifn->kif", table, filtered, precision=lax.Precision.HIGHEST)
    spectra = spectra.reshape(2, half, inputs_dev, frames_dev)
    mixed = lax.all_to_all(spectra, ("inp", "tm"), split_axis=1, concat_axis=2, tiled=True)
    n_inp = lax.axis_size("inp")
    n_tm = lax.axis_size("tm")
    owned_ch = mixed.shape[1]
    mixed = mixed.reshape(2, owned_ch, n_inp, n_tm, inputs_dev, frames_dev)
    mixed = jnp.transpose(mixed, (0, 1, 2, 4, 3, 5))
    owned = mixed.reshape(2, owned_ch, n_inp * inputs_dev, n_tm * frames_dev)
    spec_re = owned[0]
    spec_im = owned[1]
    spectra_all = spec_re.shape[2]
    plain = jnp.concatenate([spec_re, spec_im], axis=-1)
    turned = jnp.concatenate([spec_im, -spec_re], axis=-1)
    real_part = correlate_pair(plain, plain)
    imag_part = correlate_pair(turned, plain)
    return jnp.stack([real_part, imag_part]) / spectra_all


def solution(mesh):
    placed = (P("inp", "tm", None), P())
    return jax.shard_map(
        on_device,
        mesh=mesh,
        in_specs=placed,
        out_specs=P(None, ("inp", "tm"), None, None),
        check_vma=False,
    )
```

profile of v0, /device:TPU:0, one launch (start us, length us, event | category | flops | bytes accessed | tf_op | source)
XLA Modules:
  0.0 911.3 jit_solution(16799917457807516725)
XLA Ops:
  0.0 1.9 slice.33
  2.4 2.4 collective-permute-start
  4.8 0.9 fusion.42
  5.7 34.0 %sine_negate_fusion = (f32[1024,2048]{1,0:T(8,128)S(1)}, f32[1024,2048]{1,0:T(8,128)}) fusion(), kind=kLoop, calls=%fused_computation.36 | loop fusion | flops 31457280 | bytes 16777216 | tf_op jit(solution)/shard_map/neg | solution.py:21
  39.7 0.5 copy.8
  40.2 124.7 %fusion.5 = f32[2048,32,64]{0,2,1:T(8,128)} fusion(f32[32,64,2048]{2,1,0:T(8,128)} %param.2, f32[32,3,2048]{2,1,0:T(4,128)S(1)} %copy.8, f32[1024,2048]{1,0:T(8,128)S(1)} %get-tuple-element.13, f32[1024,2048]{1,0:T(8,128)} %get-tuple-element.14, f32[2048]{0:T(1024)S(1)} %bitcast.32, f32[2048]{0:T(1024)S(1)} %bitcast.33, f32[2048]{0:T(1024)S(1)} %bitcast.31, ...), kind=kOutput, calls=%fused_computation.9 | convolution fusion | flops 103129546752 | bytes 51150848 | tf_op jit(solution)/shard_map/kn,ifn->kif/dot_general | solution.py:40
  165.0 22.0 %reshape.16 = f32[2,1024,32,64]{1,0,3,2:T(2,128)} reshape(f32[2048,32,64]{0,2,1:T(8,128)} %fusion.5) | data formatting | bytes 33554432 | tf_op jit(solution)/shard_map/reshape | solution.py:41
  187.0 31.1 %copy.9 = f32[2,1024,32,64]{3,2,0,1:T(8,128)} copy(f32[2,1024,32,64]{1,0,3,2:T(2,128)} %reshape.16) | data formatting | bytes 33554432 | tf_op jit(solution)/shard_map/reshape | solution.py:41
  218.1 35.6 %reshape.19 = f32[32,1,131072]{2,1,0:T(1,128)} reshape(f32[1024,2,32,64]{3,2,1,0:T(8,128)} %bitcast.27) | data formatting | bytes 33554432
  253.7 370.5 %all_to_all.15 = f32[32,1,131072]{2,1,0:T(1,128)} all-to-all(f32[32,1,131072]{2,1,0:T(1,128)} %reshape.19), channel_id=1, replica_groups=mesh['inp'=8,'tm'=4] {'inp','tm'}, dimensions={0} | all-to-all | bytes 33554432 | tf_op jit(solution)/shard_map/all_to_all | solution.py:42
  624.2 0.5 broadcast.13
  624.8 48.3 %reduce = f32[32,131072]{1,0:T(8,128)} reduce(f32[32,1,131072]{2,1,0:T(1,128)} %all_to_all.15, f32[]{:T(128)} %broadcast.13), dimensions={1}, to_apply=%all_to_all.11.reduce_sub_computation | reduce | bytes 33554436 | tf_op jit(solution)/shard_map/all_to_all | solution.py:42
  673.1 34.7 %reshape.20 = f32[1024,2,32,64]{3,2,1,0:T(8,128)} reshape(f32[32,131072]{1,0:T(8,128)} %reduce) | data formatting | bytes 33554432
  707.8 23.7 %copy.11 = f32[2,32,32,32,64]{4,3,2,1,0:T(8,128)} copy(f32[2,32,32,32,64]{4,3,0,1,2:T(8,128)} %bitcast.29) | data formatting | bytes 33554432 | tf_op jit(solution)/shard_map/all_to_all | solution.py:42
  731.5 17.3 %fusion.40 = (f32[1,32,8,32,4,64]{5,3,4,2,1,0:T(8,128)S(1)}, f32[1,32,8,32,4,64]{5,3,4,2,1,0:T(8,128)}) fusion(f32[2,32,8,32,4,64]{5,3,4,2,1,0:T(8,128)} %bitcast.28), kind=kLoop, calls=%fused_computation.48 | loop fusion | bytes 33554432 | tf_op jit(solution)/shard_map/slice | solution.py:50
  748.8 15.4 %copy.13 = f32[1,32,8,32,4,64]{5,4,3,2,1,0:T(4,128)} copy(f32[1,32,8,32,4,64]{5,3,4,2,1,0:T(8,128)S(1)} %get-tuple-element.5) | data formatting | bytes 16777216 | tf_op jit(solution)/shard_map/slice | solution.py:50
  764.2 15.9 %squeeze.7 = f32[32,256,256]{2,1,0:T(8,128)} reshape(f32[1,32,8,32,4,64]{5,4,3,2,1,0:T(4,128)} %copy.13) | data formatting | bytes 16777216 | tf_op jit(solution)/shard_map/squeeze | solution.py:50
  780.1 21.1 %copy.12 = f32[1,32,8,32,4,64]{5,4,3,2,1,0:T(4,128)} copy(f32[1,32,8,32,4,64]{5,3,4,2,1,0:T(8,128)} %get-tuple-element.6) | data formatting | bytes 16777216 | tf_op jit(solution)/shard_map/slice | solution.py:49
  801.2 15.9 %squeeze.6 = f32[32,256,256]{2,1,0:T(8,128)} reshape(f32[1,32,8,32,4,64]{5,4,3,2,1,0:T(4,128)} %copy.12) | data formatting | bytes 16777216 | tf_op jit(solution)/shard_map/squeeze | solution.py:49
  817.1 11.4 %fusion.41 = (f32[32,256,256]{2,1,0:T(8,128)}, f32[32,256,512]{2,1,0:T(8,128)}) fusion(f32[32,256,256]{2,1,0:T(8,128)} %squeeze.6), kind=kLoop, calls=%fused_computation.49 | loop fusion | flops 2097151 | bytes 25165824 | tf_op jit(solution)/shard_map/neg | solution.py:53
  828.5 7.7 constant_dynamic-update-slice_fusion
  836.1 23.4 %convolution_bitcast_fusion = f32[1,32,256,256]{3,2,1,0:T(8,128)} fusion(f32[32,256,512]{2,1,0:T(8,128)} %constant_dynamic-update-slice_fusion), kind=kOutput, calls=%fused_computation.41 | convolution fusion | flops 12884901888 | bytes 25165824 | tf_op jit(solution)/shard_map/cas,cbs->cab/dot_general | solution.py:25
  859.6 41.9 %fusion.34 = f32[1,32,256,256]{3,2,1,0:T(8,128)} fusion(f32[32,256,512]{2,1,0:T(8,128)} %constant_dynamic-update-slice_fusion, f32[32,256,256]{2,1,0:T(8,128)} %get-tuple-element.7, f32[32,256,256]{2,1,0:T(8,128)} %squeeze.7), kind=kOutput, calls=%fused_computation.42 | convolution fusion | flops 12889096192 | bytes 41943040 | tf_op jit(solution)/shard_map/cas,cbs->cab/dot_general | solution.py:25
  901.5 9.6 %maximum_multiply_fusion.1 = f32[2,32,256,256]{3,2,1,0:T(8,128)} fusion(f32[1,32,256,256]{3,2,1,0:T(8,128)} %fusion.34, f32[1,32,256,256]{3,2,1,0:T(8,128)S(1)} %copy-done), kind=kLoop, calls=%fused_computation.23 | loop fusion | flops 8388608 | bytes 33554432 | tf_op jit(solution)/shard_map/div | solution.py:56
  (4 shorter events, 0.5 us)
Async XLA Ops:
  2.4 37.3 %collective-permute-start = (f32[32,3,2048]{2,0,1:T(8,128)S(1)}, f32[32,3,2048]{2,0,1:T(8,128)S(1)}, u32[]{:S(2)}, u32[]{:S(2)}) collective-permute-start(f32[32,3,2048]{2,0,1:T(8,128)S(1)} %copy.15), channel_id=1, source_target_pairs={{0,1},{1,2},{2,3},{4,5},{5,6},{6,7},{8,9},{9,10},{10,11},{12,13},{... | collective-permute-start | bytes 2359304 | tf_op jit(solution)/shard_map/ppermute | solution.py:12
  859.6 41.9 %copy-start = (f32[1,32,256,256]{3,2,1,0:T(8,128)S(1)}, f32[1,32,256,256]{3,2,1,0:T(8,128)}, u32[]{:S(2)}) copy-start(f32[1,32,256,256]{3,2,1,0:T(8,128)} %convolution_bitcast_fusion) | copy-start | bytes 25165828
where the time goes:
time: 918 us; the launch traced here: 911 us
  blocking collectives  370 us (40%)
  local copies, waits for them, and re-layouts  245 us (27%)
  matrix products  190 us (21%)
  other arithmetic  103 us (11%)
    all_to_all x1, blocking collectives, on_device(): lax.all_to_all(spectra, ('inp', 'tm'), split_axis=1, concat_axis=2, tiled...  370 us
    dot_general x1, matrix products, on_device(): jnp.einsum('kn,ifn->kif', table, filtered, precision=lax.Precision.HIGHEST)  125 us
    unnamed x5, local copies, waits for them, and re-layouts  70.8 us
    dot_general x2, matrix products, correlate_pair(): jnp.einsum('cas,cbs->cab', rows, cols, precision=lax.Precision.HIGHEST)  65.3 us
    reshape x2, local copies, waits for them, and re-layouts, on_device(): spectra = spectra.reshape(2, half, inputs_dev, frames_dev)  53.2 us
    all_to_all x1, other arithmetic, on_device(): lax.all_to_all(spectra, ('inp', 'tm'), split_axis=1, concat_axis=2, tiled...  48.3 us
    neg x1, other arithmetic, transform_table(): return jnp.concatenate([jnp.cos(angle), -jnp.sin(angle)], axis=0) * scale  34 us
    slice x2, local copies, waits for them, and re-layouts, on_device(): spec_im = owned[1]  32.7 us
  transfers between devices with their start and end apart: 1, of which 0 were waited for; matrix products, arithmetic and copies ran while one was open for 4% of the time, Pallas kernels for 0%

commit v1 on v0

v1 whole, which is shorter than its diff:
```python
import functools
import math

import jax
import jax.numpy as jnp
import ml_dtypes
import numpy as np
from jax import lax
from jax.experimental import pallas as pl
from jax.experimental.pallas import tpu as pltpu
from jax.sharding import PartitionSpec as P

AXES = ("inp", "tm")
GROUP = 8
BLOCK = 8
ROWS = GROUP * BLOCK
LANES = 128
PAIR = 16
VMEM_BYTES = 56 * 1024 * 1024
NT = (((1,), (1,)), ((), ()))


def fold_of(step, residue):
    if step % 4 == 0 and residue % 4 == 0:
        return "sum4"
    if step % 4 == 0 and residue % 4 == 2:
        return "alt4"
    if step % 2 == 0 and residue % 2 == 1:
        return "diff2"
    return "none"


def fold_terms(nfft, fold):
    return {"sum4": nfft // 4, "alt4": nfft // 4, "diff2": nfft // 2, "none": nfft}[fold]


def transform_table(nfft, ch_dev, count, step, residue):
    depth = fold_terms(nfft, fold_of(step, residue))
    dest = np.arange(count)[:, None]
    channel = dest * ch_dev + step * np.arange(GROUP)[None, :] + residue
    phase = channel[:, :, None] * np.arange(depth)[None, None, :] % nfft
    angle = 2.0 * math.pi / nfft * phase.astype(np.float64)
    scale = 1.0 / math.sqrt(nfft)
    table = np.concatenate([np.cos(angle), -np.sin(angle)], axis=1) * scale
    high = table.astype(ml_dtypes.bfloat16)
    low = (table - high.astype(np.float64)).astype(ml_dtypes.bfloat16)
    return high, low


def split(value):
    high = value.astype(jnp.bfloat16)
    return high, (value - high.astype(jnp.float32)).astype(jnp.bfloat16)


def dot_nt(a, b):
    return lax.dot_general(a, b, dimension_numbers=NT, preferred_element_type=jnp.float32)


def swap_halves(lane, a, b, width):
    first = lane % (2 * width) < width
    return (
        jnp.where(first, a, pltpu.roll(b, width, 1)),
        jnp.where(first, pltpu.roll(a, LANES - width, 1), b),
    )


def transform_kernel(folds, tiles, has_base, has_tail, taps_ref, *rest):
    x_refs, rest = rest[:tiles], rest[tiles:]
    before_refs, rest = rest[:tiles], rest[tiles:]
    tables, rest = rest[: 2 * len(folds)], rest[2 * len(folds) + has_base :]
    out, rest = rest[0], rest[1:]
    if has_tail:
        tail, rest = rest[0], rest[1:]
    folded, head = rest[: 2 * len(folds)], rest[2 * len(folds)]
    block, frames, _ = x_refs[0].shape
    count = out.shape[0]
    taps = taps_ref.shape[0]
    past = taps - 1
    quarter = tiles // 4

    if has_tail:

        for i in range(block):
            for tile in range(tiles):
                for r in range(past):
                    row = x_refs[tile][i, frames - past + r : frames - past + r + 1, :]
                    tail[i * past + r : i * past + r + 1, tile * LANES : (tile + 1) * LANES] = row

    def weights(tile):
        columns = slice(tile * LANES, (tile + 1) * LANES)
        return [taps_ref[k : k + 1, columns] for k in range(taps)]

    def fill_head(slot, i, tile):
        if has_tail:
            head[slot, 0:8, :] = before_refs[tile][i]
        else:
            for r in range(past):
                head[slot, 8 - past + r : 9 - past + r, :] = before_refs[tile][pl.ds(i * past + r, 1), :]
        head[slot, 8 : 8 + PAIR, :] = x_refs[tile][i, 0:PAIR, :]

    def window(slot, i, tile, start):
        if start < taps:
            return head[slot, pl.ds(8 + start, 8, stride=2), :]
        return x_refs[tile][i, pl.ds(start, 8, stride=2), :]

    def filtered(slot, i, tile, first, tap_rows):
        loads = [window(slot, i, tile, first + 1 - back) for back in range(taps + 1)]
        halves = []
        for odd in (0, 1):
            total = tap_rows[taps - 1] * loads[1 - odd]
            for back in range(1, taps):
                total = total + tap_rows[taps - 1 - back] * loads[1 - odd + back]
            halves.append(total)
        return jnp.concatenate(halves, axis=0)

    def store(which, rows, tile, value):
        high, low = split(value)
        columns = slice(tile * LANES, (tile + 1) * LANES)
        folded[2 * which][rows, columns] = high
        folded[2 * which + 1][rows, columns] = low

    for tile in range(tiles if "none" in folds else quarter):
        sources = [tile] if "none" in folds else [tile + q * quarter for q in range(4)]

        @pl.loop(0, block)
        def _(i):
            tap_rows = [weights(source) for source in sources]
            for slot, source in enumerate(sources):
                fill_head(slot, i, source)
            for first in range(0, frames, PAIR):
                rows = pl.ds(pl.multiple_of(i * frames + first, PAIR), PAIR)
                f = [
                    filtered(slot, i, source, first, tap_rows[slot])
                    for slot, source in enumerate(sources)
                ]
                for which, fold in enumerate(folds):
                    if fold == "none":
                        store(which, rows, tile, f[0])
                    elif fold == "sum4":
                        store(which, rows, tile, (f[0] + f[2]) + (f[1] + f[3]))
                    elif fold == "alt4":
                        store(which, rows, tile, (f[0] + f[2]) - (f[1] + f[3]))
                    else:
                        store(which, rows, tile, f[0] - f[2])
                        store(which, rows, tile + quarter, f[1] - f[3])

    lane = lax.broadcasted_iota(jnp.int32, (GROUP, LANES), 1)
    together = min(16, count)
    for start in range(0, count, together):
        rows = slice(start * 2 * GROUP, (start + together) * 2 * GROUP)
        specs = []
        for which in range(len(folds)):
            a_hi, a_lo = tables[2 * which][rows], tables[2 * which + 1][rows]
            g_hi, g_lo = folded[2 * which], folded[2 * which + 1]
            specs.append(dot_nt(a_hi, g_hi[...]) + dot_nt(a_lo, g_hi[...]) + dot_nt(a_hi, g_lo[...]))
        for k in range(together):
            top = 2 * GROUP * k
            parts = [s[top + h * GROUP : top + (h + 1) * GROUP] for s in specs for h in (0, 1)]
            for at in range(0, block * frames // LANES):
                tiles_at = [p[:, at * LANES : (at + 1) * LANES] for p in parts]
                if len(parts) == 2:
                    mixed = swap_halves(lane, tiles_at[0], tiles_at[1], LANES // 2)
                else:
                    u0, u2 = swap_halves(lane, tiles_at[0], tiles_at[2], LANES // 2)
                    u1, u3 = swap_halves(lane, tiles_at[1], tiles_at[3], LANES // 2)
                    mixed = swap_halves(lane, u0, u1, LANES // 4) + swap_halves(lane, u2, u3, LANES // 4)
                for j, tile in enumerate(mixed):
                    i = at * len(parts) + j
                    out[start + k, pl.ds(i, GROUP, stride=block), :] = tile


def transform(voltages, before, filter_taps, count, ch_dev, step, residues, half, span, size, at, base=None):
    inputs_dev, frames, nfft = voltages.shape
    past = filter_taps.shape[0] - 1
    folds = [fold_of(step, residue) for residue in residues]
    tiles = nfft // LANES
    if half is not None:
        frames = frames // 2
    low, high = span
    blocks = high - low
    has_base = int(base is not None)
    has_tail = half == 1
    operands = []
    specs = []

    def add(operand, spec):
        operands.append(operand)
        specs.append(spec)

    add(filter_taps, pl.BlockSpec(filter_taps.shape, lambda b: (0, 0)))
    for tile in range(tiles):
        add(voltages, pl.BlockSpec((BLOCK, frames, LANES), lambda b, t=tile: (b + low, half or 0, t)))
    for tile in range(tiles):
        if has_tail:
            add(
                voltages,
                pl.BlockSpec((BLOCK, 8, LANES), lambda b, t=tile: (b + low, frames // 8 - 1, t)),
            )
        else:
            add(before, pl.BlockSpec((BLOCK * past, LANES), lambda b, t=tile: (b + low, t)))
    scratch = []
    flops = 0
    for residue, fold in zip(residues, folds):
        depth = fold_terms(nfft, fold)
        for table in transform_table(nfft, ch_dev, count, step, residue):
            table = table.reshape(-1, depth)
            add(
                jnp.asarray(table),
                pl.BlockSpec(table.shape, lambda b: (0, 0), pipeline_mode=pl.Buffered(1)),
            )
        scratch += [pltpu.VMEM((BLOCK * frames, depth), jnp.bfloat16)] * 2
        flops += 6 * 2 * GROUP * count * depth * blocks * BLOCK * frames
    scratch.append(pltpu.VMEM((4, 8 + PAIR, LANES), jnp.float32))
    aliases = {}
    if has_base:
        aliases[len(operands)] = 0
        add(base, pl.BlockSpec(memory_space=pl.ANY))
    shapes = [jax.ShapeDtypeStruct((count, size * ROWS, LANES), jnp.float32)]
    out_specs = [pl.BlockSpec((count, ROWS, LANES), lambda b: (0, b + at, 0))]
    if has_tail:
        shapes.append(jax.ShapeDtypeStruct((blocks * BLOCK * past, nfft), jnp.float32))
        out_specs.append(pl.BlockSpec((BLOCK * past, nfft), lambda b: (b, 0)))
    return pl.pallas_call(
        functools.partial(transform_kernel, folds, tiles, has_base, has_tail),
        grid=(blocks,),
        out_shape=shapes,
        input_output_aliases=aliases,
        in_specs=specs,
        out_specs=out_specs,
        scratch_shapes=scratch,
        compiler_params=pltpu.CompilerParams(vmem_limit_bytes=VMEM_BYTES),
        cost_estimate=pl.CostEstimate(
            flops=flops, bytes_accessed=4 * blocks * BLOCK * frames * nfft, transcendentals=0
        ),
        name="spectra_" + "_".join(map(str, residues)) + ("" if half is None else f"_half{half}"),
    )(*operands)


def correlate_kernel(n_inp, n_tm, frames, pieces, together, has_base, *rest):
    streams = []
    for number in pieces:
        streams.append(rest[:number])
        rest = rest[number:]
    (out,) = rest[has_base:]
    scale = 1.0 / (n_tm * frames)
    width = LANES // 2 // len(pieces)
    first = lax.broadcasted_iota(jnp.int32, (1, LANES), 1) % (2 * width) < width
    low_half = lax.broadcasted_iota(jnp.int32, (1, LANES), 1) < LANES // 2

    def payload(stream, sender, c):
        rows = slice(c * BLOCK, (c + 1) * BLOCK)
        return [
            array[sender, b, rows, :] for array in streams[stream] for b in range(array.shape[1])
        ]

    for c in range(together):
        columns = []
        for t in range(n_tm):
            senders = [p * n_tm + t for p in range(n_inp)]
            value = jnp.concatenate([x for s in senders for x in payload(0, s, c)], axis=0)
            if len(pieces) == 1:
                turned = pltpu.roll(value, width, 1)
                turned = jnp.where(first, turned, -turned)
            else:
                other = jnp.concatenate([x for s in senders for x in payload(1, s, c)], axis=0)
                turn = pl.program_id(1) * (LANES // 2)
                value = jnp.where(
                    low_half, pltpu.roll(value, turn, 1), pltpu.roll(other, LANES // 2 - turn, 1)
                )
                turned = jnp.where(
                    first, pltpu.roll(value, LANES - width, 1), -pltpu.roll(value, width, 1)
                )
            columns.append(split(value) + split(turned))
        p_hi, p_lo, t_hi, t_lo = [jnp.concatenate(column, axis=1) for column in zip(*columns)]
        right = jnp.concatenate([p_hi, p_hi, p_lo], axis=1)
        out[0, c, 0] = dot_nt(jnp.concatenate([p_hi, p_lo, p_hi], axis=1), right) * scale
        out[1, c, 0] = dot_nt(jnp.concatenate([t_hi, t_lo, t_hi], axis=1), right) * scale


def correlate(streams, base, n_inp, n_tm, inputs_dev, frames, ch_dev, step, residues):
    count = n_inp * n_tm
    n_inputs = n_inp * inputs_dev
    has_base = int(base is not None)
    together = 2
    operands = []
    specs = []
    for stream in streams:
        for array, number, at in stream:
            operands.append(array.reshape(count, -1, ROWS, LANES))
            specs.append(
                pl.BlockSpec(
                    (count, number, together * BLOCK, LANES),
                    lambda c, r, q=at // number: (0, q, c, 0),
                )
            )
    aliases = {}
    if has_base:
        aliases[len(operands)] = 0
        operands.append(base)
        specs.append(pl.BlockSpec(memory_space=pl.ANY))
    gap = residues[-1] - residues[0]
    pieces = [len(stream) for stream in streams]
    size = GROUP * len(residues)
    return pl.pallas_call(
        functools.partial(correlate_kernel, n_inp, n_tm, frames, pieces, together, has_base),
        grid=(GROUP // together, len(residues)),
        out_shape=jax.ShapeDtypeStruct((2, GROUP, step, n_inputs, n_inputs), jnp.float32),
        in_specs=specs,
        out_specs=pl.BlockSpec(
            (2, together, 1, n_inputs, n_inputs), lambda c, r: (0, c, residues[0] + gap * r, 0, 0)
        ),
        input_output_aliases=aliases,
        compiler_params=pltpu.CompilerParams(vmem_limit_bytes=VMEM_BYTES),
        cost_estimate=pl.CostEstimate(
            flops=12 * size * n_inputs * n_inputs * n_tm * LANES,
            bytes_accessed=4 * size * (n_inputs * n_tm * LANES + 2 * n_inputs * n_inputs),
            transcendentals=0,
        ),
        name="correlate_" + "_".join(map(str, residues)),
    )(*operands)


def on_device(voltages, filter_taps):
    inputs_dev, frames, nfft = voltages.shape
    n_inp = lax.axis_size("inp")
    n_tm = lax.axis_size("tm")
    count = n_inp * n_tm
    ch_dev = nfft // 2 // count
    step = ch_dev // GROUP
    blocks = inputs_dev // BLOCK

    def history(tail):
        return lax.ppermute(tail, "tm", [(t, t + 1) for t in range(n_tm - 1)])

    def exchange(payload):
        return lax.all_to_all(payload, AXES, split_axis=0, concat_axis=0, tiled=True)

    def spectra(before, residues, half, *places):
        return transform(voltages, before, filter_taps, count, ch_dev, step, residues, half, *places)

    def visibilities(streams, base, residues):
        return correlate(streams, base, n_inp, n_tm, inputs_dev, frames, ch_dev, step, residues)

    everything = (0, blocks)
    if step != 4 or blocks % 4:
        past = filter_taps.shape[0] - 1
        before = history(voltages[:, frames - past :, :].reshape(-1, nfft))
        result = None
        for residue in range(step):
            (sent,) = spectra(before, [residue], None, everything, blocks, 0)
            result = visibilities([[(exchange(sent), blocks, 0)]], result, [residue])
        return result.reshape(2, ch_dev, *result.shape[3:])

    rest = blocks - 1
    first, tail_first = spectra(None, [0, 2], 1, (0, 1), 1, 0)
    got_first = exchange(first)
    second, tail_rest = spectra(None, [0, 2], 1, (1, blocks), rest, 0)
    before = history(jnp.concatenate([tail_first, tail_rest], axis=0))
    got_second = exchange(second)
    (third,) = spectra(before, [0, 2], 0, everything, 2 * blocks, 0)
    (third,) = spectra(before, [1], None, everything, 2 * blocks, blocks, third)
    got_third = exchange(third)
    (fourth,) = spectra(before, [3], None, everything, blocks, 0)
    got_fourth = exchange(fourth)
    late = [(got_first, 1, 0), (got_second, rest, 0)]
    early = [(got_third, blocks, 0)]
    result = visibilities([late, early], None, [0, 2])
    result = visibilities([[(got_third, blocks, blocks)]], result, [1])
    result = visibilities([[(got_fourth, blocks, 0)]], result, [3])
    return result.reshape(2, ch_dev, *result.shape[3:])


def solution(mesh):
    return jax.shard_map(
        on_device,
        mesh=mesh,
        in_specs=(P("inp", "tm", None), P()),
        out_specs=P(None, AXES, None, None),
        check_vma=False,
    )
```

time: 918 us -> 415 us (0.45)
  blocking collectives: 370 us -> 0 us
  waiting for transfers between devices: 0.01 us -> 285 us
  local copies, waits for them, and re-layouts: 245 us -> 0.95 us
  matrix products: 190 us -> 0 us
  other arithmetic: 103 us -> 1.12 us
  Pallas kernels: 0 us -> 101 us
  starting transfers between devices: 2.41 us -> 25.5 us
    all_to_all x1 -> x0, blocking collectives: 370 us -> none  [on_device(): lax.all_to_all(spectra, ('inp', 'tm'), split_axis=1, concat_axis=2, tiled...]
    all_to_all x0 -> x4, waiting for transfers between devices: none -> 283 us  [exchange(): lax.all_to_all(payload, AXES, split_axis=0, concat_axis=0, tiled=True)]
    dot_general x3 -> x0, matrix products: 190 us -> none  [the longest x1 125 us: on_device(): jnp.einsum('kn,ifn->kif', table, filtered, precision=lax.Precision.HIGHEST)]
    pallas_call x0 -> x8, Pallas kernels: none -> 101 us  [the longest x5 70.7 us: transform(): pl.pallas_call(functools.partial(transform_kernel, folds, tiles, has_base...]
    unnamed x5 -> x4, local copies, waits for them, and re-layouts: 70.8 us -> 0.95 us
    slice x5 -> x0, local copies, waits for them, and re-layouts: 56.6 us -> none  [the longest x2 32.7 us: on_device(): spec_im = owned[1]]
    reshape x2 -> x0, local copies, waits for them, and re-layouts: 53.2 us -> none  [on_device(): spectra = spectra.reshape(2, half, inputs_dev, frames_dev)]
    all_to_all x1 -> x0, other arithmetic: 48.3 us -> none  [on_device(): lax.all_to_all(spectra, ('inp', 'tm'), split_axis=1, concat_axis=2, tiled...]
  transfers between devices with their start and end apart: 1 -> 5, of which waited for: 0 -> 5; matrix products, arithmetic and copies ran while one was open for 4% -> 0% of each run, Pallas kernels for 0% -> 21%
where the time goes in v1:
time: 415 us; the launch traced here: 414 us
  waiting for transfers between devices  285 us (69%)
  Pallas kernels  101 us (24%)
  starting transfers between devices  25.5 us (6%)
    all_to_all x4, waiting for transfers between devices, exchange(): lax.all_to_all(payload, AXES, split_axis=0, concat_axis=0, tiled=True)  283 us
    pallas_call x5, Pallas kernels, transform(): pl.pallas_call(functools.partial(transform_kernel, folds, tiles, has_base...  70.7 us
    pallas_call x3, Pallas kernels, correlate(): pl.pallas_call(functools.partial(correlate_kernel, n_inp, n_tm, frames, p...  30.5 us
    all_to_all x4, starting transfers between devices, exchange(): lax.all_to_all(payload, AXES, split_axis=0, concat_axis=0, tiled=True)  23.4 us
  transfers between devices with their start and end apart: 5, of which 5 were waited for; matrix products, arithmetic and copies ran while one was open for 0% of the time, Pallas kernels for 21%

profile of v1, /device:TPU:0, one launch (start us, length us, event | category | flops | bytes accessed | tf_op | source)
XLA Modules:
  0.0 414.0 jit_solution(10951960349612948386)
XLA Ops:
  0.0 6.0 %spectra_0_2_half1.2 = (f32[32,64,128]{2,1,0:T(8,128)}, f32[24,2048]{1,0:T(8,128)}) custom-call(f32[4,2048]{1,0:T(4,128)} %taps_ref.9, f32[32,64,2048]{2,1,0:T(8,128)} %rest_15_.9, f32[32,64,2048]{2,1,0:T(8,128)} %rest_15_.9, f32[32,64,2048]{2,1,0:T(8,128)} %rest_15_.9, f32[32,64,2048]{2,1,0:T(8,128)} %rest_15_.9, f32[32,64,2048]{2,1,0:T(8,128)} %rest_15_.9, ...), custom_call_target="tpu_custom_call" | custom-call | flops 805306368 | bytes 2097152 | tf_op jit(solution)/shard_map/spectra_0_2_half1/pallas_call | solution.py:223
  6.0 7.4 %all-to-all-start.2 = ((f32[32,64,128]{2,1,0:T(8,128)}), f32[32,64,128]{2,1,0:T(8,128)}, u32[]{:S(2)}, u32[]{:S(2)}) async-start(f32[32,64,128]{2,1,0:T(8,128)} %get-tuple-element.11), calls=%async_computation.2 | async-start | bytes 2097152 | tf_op jit(solution)/shard_map/all_to_all | solution.py:336
  13.5 0.0 copy-start.1
  13.5 11.7 %spectra_0_2_half1.3 = (f32[32,192,128]{2,1,0:T(8,128)}, f32[72,2048]{1,0:T(8,128)}) custom-call(f32[4,2048]{1,0:T(4,128)} %taps_ref.9, f32[32,64,2048]{2,1,0:T(8,128)} %rest_15_.9, f32[32,64,2048]{2,1,0:T(8,128)} %rest_15_.9, f32[32,64,2048]{2,1,0:T(8,128)} %rest_15_.9, f32[32,64,2048]{2,1,0:T(8,128)} %rest_15_.9, f32[32,64,2048]{2,1,0:T(8,128)} %rest_15_.9, ...), custom_call_target="tpu_custom_call" | custom-call | flops 2415919104 | bytes 6291456 | tf_op jit(solution)/shard_map/spectra_0_2_half1/pallas_call | solution.py:223
  25.2 14.5 %all-to-all-done.2 = f32[32,64,128]{2,1,0:T(8,128)} async-done(((f32[32,64,128]{2,1,0:T(8,128)}), f32[32,64,128]{2,1,0:T(8,128)}, u32[]{:S(2)}, u32[]{:S(2)}) %all-to-all-start.2) | async-done | bytes 1048608 | tf_op jit(solution)/shard_map/all_to_all | solution.py:336
  39.7 3.7 all-to-all-start.3
  43.4 0.0 copy-done.1
  43.4 1.1 pad_maximum_fusion
  44.5 2.1 collective-permute-start
  46.7 1.8 collective-permute-done.rest_16_.rest_17_.rest_18_.rest_19_.rest_20_.rest_21_.rest_22_.rest_23_.rest_24_.rest_25_.rest_26_.rest_27_.rest_28_.rest_29_.rest_30_.rest_31_
  48.5 0.0 copy-start
  48.5 0.9 copy-done
  49.5 13.9 %spectra_0_2_half0.1.rest_34_ = f32[32,512,128]{2,1,0:T(8,128)} custom-call(f32[4,2048]{1,0:T(4,128)} %taps_ref.9, f32[32,64,2048]{2,1,0:T(8,128)} %rest_15_.9, f32[32,64,2048]{2,1,0:T(8,128)} %rest_15_.9, f32[32,64,2048]{2,1,0:T(8,128)} %rest_15_.9, f32[32,64,2048]{2,1,0:T(8,128)} %rest_15_.9, f32[32,64,2048]{2,1,0:T(8,128)} %rest_15_.9, ...), custom_call_target="tpu_custom_call" | custom-call | flops 3221225472 | bytes 8388608 | tf_op jit(solution)/shard_map/spectra_0_2_half0/pallas_call | solution.py:223
  63.4 19.5 %spectra_1.1 = f32[32,512,128]{2,1,0:T(8,128)} custom-call(f32[4,2048]{1,0:T(4,128)} %taps_ref.9, f32[32,64,2048]{2,1,0:T(8,128)} %rest_15_.9, f32[32,64,2048]{2,1,0:T(8,128)} %rest_15_.9, f32[32,64,2048]{2,1,0:T(8,128)} %rest_15_.9, f32[32,64,2048]{2,1,0:T(8,128)} %rest_15_.9, f32[32,64,2048]{2,1,0:T(8,128)} %rest_15_.9, ...), custom_call_target="tpu_custom_call", output_to_operand_aliasing={{}: (35, {})} | custom-call | flops 6442450944 | bytes 16777216 | tf_op jit(solution)/shard_map/spectra_1/pallas_call | solution.py:223
  82.9 32.2 %all-to-all-done.3 = f32[32,192,128]{2,1,0:T(8,128)} async-done(((f32[32,192,128]{2,1,0:T(8,128)}), f32[32,192,128]{2,1,0:T(8,128)}, u32[]{:S(2)}, u32[]{:S(2)}) %all-to-all-start.3) | async-done | bytes 3145760 | tf_op jit(solution)/shard_map/all_to_all | solution.py:336
  115.1 4.6 %all-to-all-start.1 = ((f32[32,512,128]{2,1,0:T(8,128)}), f32[32,512,128]{2,1,0:T(8,128)}, u32[]{:S(2)}, u32[]{:S(2)}) async-start(f32[32,512,128]{2,1,0:T(8,128)} %spectra_1.1), calls=%async_computation.1 | async-start | bytes 16777216 | tf_op jit(solution)/shard_map/all_to_all | solution.py:336
  119.8 19.5 %spectra_3.1 = f32[32,256,128]{2,1,0:T(8,128)} custom-call(f32[4,2048]{1,0:T(4,128)} %taps_ref.9, f32[32,64,2048]{2,1,0:T(8,128)} %rest_15_.9, f32[32,64,2048]{2,1,0:T(8,128)} %rest_15_.9, f32[32,64,2048]{2,1,0:T(8,128)} %rest_15_.9, f32[32,64,2048]{2,1,0:T(8,128)} %rest_15_.9, f32[32,64,2048]{2,1,0:T(8,128)} %rest_15_.9, f32[32,64,2048]{2,1,0:T(8,128)} %rest_15_.9, ...), custom_call_target="tpu_custom_call" | custom-call | flops 6442450944 | bytes 16777216 | tf_op jit(solution)/shard_map/spectra_3/pallas_call | solution.py:223
  139.3 165.7 %all-to-all-done.1 = f32[32,512,128]{2,1,0:T(8,128)} async-done(((f32[32,512,128]{2,1,0:T(8,128)}), f32[32,512,128]{2,1,0:T(8,128)}, u32[]{:S(2)}, u32[]{:S(2)}) %all-to-all-start.1) | async-done | bytes 8388640 | tf_op jit(solution)/shard_map/all_to_all | solution.py:336
  305.0 7.6 %all-to-all-start = ((f32[32,256,128]{2,1,0:T(8,128)}), f32[32,256,128]{2,1,0:T(8,128)}, u32[]{:S(2)}, u32[]{:S(2)}) async-start(f32[32,256,128]{2,1,0:T(8,128)} %spectra_3.1), calls=%async_computation | async-start | bytes 8388608 | tf_op jit(solution)/shard_map/all_to_all | solution.py:336
  312.7 16.3 %correlate_0_2.1.rest_1_ = f32[2,8,4,256,256]{4,3,2,1,0:T(8,128)} custom-call(f32[32,1,64,128]{3,2,1,0:T(8,128)} %bitcast.2.rest_0_, f32[32,3,64,128]{3,2,1,0:T(8,128)} %bitcast.3.rest_1_, f32[32,8,64,128]{3,2,1,0:T(8,128)} %bitcast.1.rest_2_.rest_0_), custom_call_target="tpu_custom_call" | custom-call | flops 6442450944 | bytes 16777216 | tf_op jit(solution)/shard_map/correlate_0_2/pallas_call | solution.py:304
  329.0 7.1 %correlate_1.1.rest_1_ = f32[2,8,4,256,256]{4,3,2,1,0:T(8,128)} custom-call(f32[32,8,64,128]{3,2,1,0:T(8,128)} %bitcast.1.rest_2_.rest_0_, f32[2,8,4,256,256]{4,3,2,1,0:T(8,128)} %correlate_0_2.1.rest_1_), custom_call_target="tpu_custom_call", output_to_operand_aliasing={{}: (1, {})} | custom-call | flops 3221225472 | bytes 8388608 | tf_op jit(solution)/shard_map/correlate_1/pallas_call | solution.py:304
  336.1 70.8 %all-to-all-done = f32[32,256,128]{2,1,0:T(8,128)} async-done(((f32[32,256,128]{2,1,0:T(8,128)}), f32[32,256,128]{2,1,0:T(8,128)}, u32[]{:S(2)}, u32[]{:S(2)}) %all-to-all-start) | async-done | bytes 4194336 | tf_op jit(solution)/shard_map/all_to_all | solution.py:336
  406.9 7.1 %correlate_3.1 = f32[2,8,4,256,256]{4,3,2,1,0:T(8,128)} custom-call(f32[32,4,64,128]{3,2,1,0:T(8,128)} %bitcast.rest_0_, f32[2,8,4,256,256]{4,3,2,1,0:T(8,128)} %correlate_1.1.rest_1_), custom_call_target="tpu_custom_call", output_to_operand_aliasing={{}: (1, {})} | custom-call | flops 3221225472 | bytes 8388608 | tf_op jit(solution)/shard_map/correlate_3/pallas_call | solution.py:304
Async XLA Ops:
  6.0 33.7 %all-to-all-start.2 = ((f32[32,64,128]{2,1,0:T(8,128)}), f32[32,64,128]{2,1,0:T(8,128)}, u32[]{:S(2)}, u32[]{:S(2)}) async-start(f32[32,64,128]{2,1,0:T(8,128)} %get-tuple-element.11), calls=%async_computation.2 | async-start | bytes 2097152 | tf_op jit(solution)/shard_map/all_to_all | solution.py:336
  13.5 30.0 %copy-start.1 = (f32[24,2048]{1,0:T(8,128)S(1)}, f32[24,2048]{1,0:T(8,128)}, u32[]{:S(2)}) copy-start(f32[24,2048]{1,0:T(8,128)} %get-tuple-element.9) | copy-start | bytes 589828
  39.7 75.5 %all-to-all-start.3 = ((f32[32,192,128]{2,1,0:T(8,128)}), f32[32,192,128]{2,1,0:T(8,128)}, u32[]{:S(2)}, u32[]{:S(2)}) async-start(f32[32,192,128]{2,1,0:T(8,128)} %get-tuple-element.12), calls=%async_computation.3 | async-start | bytes 6291456 | tf_op jit(solution)/shard_map/all_to_all | solution.py:336
  44.5 4.0 collective-permute-start
  48.5 0.9 copy-start
  115.1 189.9 %all-to-all-start.1 = ((f32[32,512,128]{2,1,0:T(8,128)}), f32[32,512,128]{2,1,0:T(8,128)}, u32[]{:S(2)}, u32[]{:S(2)}) async-start(f32[32,512,128]{2,1,0:T(8,128)} %spectra_1.1), calls=%async_computation.1 | async-start | bytes 16777216 | tf_op jit(solution)/shard_map/all_to_all | solution.py:336
  305.0 101.9 %all-to-all-start = ((f32[32,256,128]{2,1,0:T(8,128)}), f32[32,256,128]{2,1,0:T(8,128)}, u32[]{:S(2)}, u32[]{:S(2)}) async-start(f32[32,256,128]{2,1,0:T(8,128)} %spectra_3.1), calls=%async_computation | async-start | bytes 8388608 | tf_op jit(solution)/shard_map/all_to_all | solution.py:336

commit v2 on v1

--- a/solution.py
+++ b/solution.py
@@ -64,38 +64,29 @@
     )
 
 
-def transform_kernel(folds, tiles, has_base, has_tail, taps_ref, *rest):
+def transform_kernel(folds, tiles, has_base, splits, taps_ref, before_ref, *rest):
     x_refs, rest = rest[:tiles], rest[tiles:]
-    before_refs, rest = rest[:tiles], rest[tiles:]
     tables, rest = rest[: 2 * len(folds)], rest[2 * len(folds) + has_base :]
-    out, rest = rest[0], rest[1:]
-    if has_tail:
-        tail, rest = rest[0], rest[1:]
+    outs, rest = rest[:splits], rest[splits:]
     folded, head = rest[: 2 * len(folds)], rest[2 * len(folds)]
     block, frames, _ = x_refs[0].shape
-    count = out.shape[0]
+    count = outs[0].shape[0]
     taps = taps_ref.shape[0]
     past = taps - 1
     quarter = tiles // 4
 
-    if has_tail:
-
-        for i in range(block):
-            for tile in range(tiles):
-                for r in range(past):
-                    row = x_refs[tile][i, frames - past + r : frames - past + r + 1, :]
-                    tail[i * past + r : i * past + r + 1, tile * LANES : (tile + 1) * LANES] = row
-
     def weights(tile):
         columns = slice(tile * LANES, (tile + 1) * LANES)
         return [taps_ref[k : k + 1, columns] for k in range(taps)]
 
     def fill_head(slot, i, tile):
-        if has_tail:
-            head[slot, 0:8, :] = before_refs[tile][i]
+        columns = slice(tile * LANES, (tile + 1) * LANES)
+        if len(before_ref.shape) == 3:
+            head[slot, 0:8, :] = before_ref[i, :, columns]
         else:
             for r in range(past):
-                head[slot, 8 - past + r : 9 - past + r, :] = before_refs[tile][pl.ds(i * past + r, 1), :]
+                row = before_ref[pl.ds(i * past + r, 1), columns]
+                head[slot, 8 - past + r : 9 - past + r, :] = row
         head[slot, 8 : 8 + PAIR, :] = x_refs[tile][i, 0:PAIR, :]
 
     def window(slot, i, tile, start):
@@ -122,7 +113,7 @@
     for tile in range(tiles if "none" in folds else quarter):
         sources = [tile] if "none" in folds else [tile + q * quarter for q in range(4)]
 
-        @pl.loop(0, block)
+        @pl.loop(0, block, unroll=block)
         def _(i):
             tap_rows = [weights(source) for source in sources]
             for slot, source in enumerate(sources):
@@ -166,10 +157,36 @@
                     mixed = swap_halves(lane, u0, u1, LANES // 4) + swap_halves(lane, u2, u3, LANES // 4)
                 for j, tile in enumerate(mixed):
                     i = at * len(parts) + j
-                    out[start + k, pl.ds(i, GROUP, stride=block), :] = tile
-
-
-def transform(voltages, before, filter_taps, count, ch_dev, step, residues, half, span, size, at, base=None):
+                    share = GROUP // splits
+                    for n, out in enumerate(outs):
+                        rows = pl.ds(i, share, stride=block)
+                        out[start + k, rows, :] = tile[n * share : (n + 1) * share]
+
+
+def last_frames_kernel(past, x_ref, _, out):
+    inputs_dev, rows, _ = x_ref.shape
+    for i in range(inputs_dev):
+        for r in range(past):
+            out[i * past + r : i * past + r + 1, :] = x_ref[i, rows - past + r : rows - past + r + 1, :]
+
+
+def last_frames(voltages, past, event):
+    inputs_dev, frames, nfft = voltages.shape
+    return pl.pallas_call(
+        functools.partial(last_frames_kernel, past),
+        grid=(1,),
+        out_shape=jax.ShapeDtypeStruct((inputs_dev * past, nfft), jnp.float32),
+        in_specs=[
+            pl.BlockSpec((inputs_dev, 8, nfft), lambda b: (0, frames // 8 - 1, 0)),
+            pl.BlockSpec(memory_space=pl.ANY),
+        ],
+        out_specs=pl.BlockSpec((inputs_dev * past, nfft), lambda b: (0, 0)),
+        compiler_params=pltpu.CompilerParams(vmem_limit_bytes=VMEM_BYTES),
+        name="last_frames",
+    )(voltages, event)
+
+
+def transform(voltages, before, filter_taps, count, ch_dev, step, residues, half, span, *places):
     inputs_dev, frames, nfft = voltages.shape
     past = filter_taps.shape[0] - 1
     folds = [fold_of(step, residue) for residue in residues]
@@ -178,8 +195,8 @@
         frames = frames // 2
     low, high = span
     blocks = high - low
+    base = places[0][2] if len(places[0]) == 3 else None
     has_base = int(base is not None)
-    has_tail = half == 1
     operands = []
     specs = []
 
@@ -188,16 +205,12 @@
         specs.append(spec)
 
     add(filter_taps, pl.BlockSpec(filter_taps.shape, lambda b: (0, 0)))
+    if half == 1:
+        add(voltages, pl.BlockSpec((BLOCK, 8, nfft), lambda b: (b + low, frames // 8 - 1, 0)))
+    else:
+        add(before, pl.BlockSpec((BLOCK * past, nfft), lambda b: (b + low, 0)))
     for tile in range(tiles):
         add(voltages, pl.BlockSpec((BLOCK, frames, LANES), lambda b, t=tile: (b + low, half or 0, t)))
-    for tile in range(tiles):
-        if has_tail:
-            add(
-                voltages,
-                pl.BlockSpec((BLOCK, 8, LANES), lambda b, t=tile: (b + low, frames // 8 - 1, t)),
-            )
-        else:
-            add(before, pl.BlockSpec((BLOCK * past, LANES), lambda b, t=tile: (b + low, t)))
     scratch = []
     flops = 0
     for residue, fold in zip(residues, folds):
@@ -215,18 +228,16 @@
     if has_base:
         aliases[len(operands)] = 0
         add(base, pl.BlockSpec(memory_space=pl.ANY))
-    shapes = [jax.ShapeDtypeStruct((count, size * ROWS, LANES), jnp.float32)]
-    out_specs = [pl.BlockSpec((count, ROWS, LANES), lambda b: (0, b + at, 0))]
-    if has_tail:
-        shapes.append(jax.ShapeDtypeStruct((blocks * BLOCK * past, nfft), jnp.float32))
-        out_specs.append(pl.BlockSpec((BLOCK * past, nfft), lambda b: (b, 0)))
+    share = ROWS // len(places)
     return pl.pallas_call(
-        functools.partial(transform_kernel, folds, tiles, has_base, has_tail),
+        functools.partial(transform_kernel, folds, tiles, has_base, len(places)),
         grid=(blocks,),
-        out_shape=shapes,
+        out_shape=[jax.ShapeDtypeStruct((count, place[0] * share, LANES), jnp.float32) for place in places],
         input_output_aliases=aliases,
         in_specs=specs,
-        out_specs=out_specs,
+        out_specs=[
+            pl.BlockSpec((count, share, LANES), lambda b, at=place[1]: (0, b + at, 0)) for place in places
+        ],
         scratch_shapes=scratch,
         compiler_params=pltpu.CompilerParams(vmem_limit_bytes=VMEM_BYTES),
         cost_estimate=pl.CostEstimate(
@@ -277,7 +288,7 @@
         out[1, c, 0] = dot_nt(jnp.concatenate([t_hi, t_lo, t_hi], axis=1), right) * scale
 
 
-def correlate(streams, base, n_inp, n_tm, inputs_dev, frames, ch_dev, step, residues):
+def correlate(streams, base, n_inp, n_tm, inputs_dev, frames, ch_dev, step, residues, channels):
     count = n_inp * n_tm
     n_inputs = n_inp * inputs_dev
     has_base = int(base is not None)
@@ -286,7 +297,7 @@
     specs = []
     for stream in streams:
         for array, number, at in stream:
-            operands.append(array.reshape(count, -1, ROWS, LANES))
+            operands.append(array.reshape(count, -1, (channels[1] - channels[0]) * BLOCK, LANES))
             specs.append(
                 pl.BlockSpec(
                     (count, number, together * BLOCK, LANES),
@@ -300,23 +311,24 @@
         specs.append(pl.BlockSpec(memory_space=pl.ANY))
     gap = residues[-1] - residues[0]
     pieces = [len(stream) for stream in streams]
-    size = GROUP * len(residues)
+    size = (channels[1] - channels[0]) * len(residues)
+    skip = channels[0] // together
     return pl.pallas_call(
         functools.partial(correlate_kernel, n_inp, n_tm, frames, pieces, together, has_base),
-        grid=(GROUP // together, len(residues)),
+        grid=((channels[1] - channels[0]) // together, len(residues)),
         out_shape=jax.ShapeDtypeStruct((2, GROUP, step, n_inputs, n_inputs), jnp.float32),
         in_specs=specs,
         out_specs=pl.BlockSpec(
-            (2, together, 1, n_inputs, n_inputs), lambda c, r: (0, c, residues[0] + gap * r, 0, 0)
+            (2, together, 1, n_inputs, n_inputs), lambda c, r: (0, c + skip, residues[0] + gap * r, 0, 0)
         ),
         input_output_aliases=aliases,
-        compiler_params=pltpu.CompilerParams(vmem_limit_bytes=VMEM_BYTES),
+        compiler_params=pltpu.CompilerParams(vmem_limit_bytes=62 * 1024 * 1024),
         cost_estimate=pl.CostEstimate(
             flops=12 * size * n_inputs * n_inputs * n_tm * LANES,
             bytes_accessed=4 * size * (n_inputs * n_tm * LANES + 2 * n_inputs * n_inputs),
             transcendentals=0,
         ),
-        name="correlate_" + "_".join(map(str, residues)),
+        name="correlate_" + "_".join(map(str, residues)) + f"_from{channels[0]}",
     )(*operands)
 
 
@@ -338,8 +350,10 @@
     def spectra(before, residues, half, *places):
         return transform(voltages, before, filter_taps, count, ch_dev, step, residues, half, *places)
 
-    def visibilities(streams, base, residues):
-        return correlate(streams, base, n_inp, n_tm, inputs_dev, frames, ch_dev, step, residues)
+    def visibilities(streams, base, residues, channels=(0, GROUP)):
+        return correlate(
+            streams, base, n_inp, n_tm, inputs_dev, frames, ch_dev, step, residues, channels
+        )
 
     everything = (0, blocks)
     if step != 4 or blocks % 4:
@@ -347,26 +361,24 @@
         before = history(voltages[:, frames - past :, :].reshape(-1, nfft))
         result = None
         for residue in range(step):
-            (sent,) = spectra(before, [residue], None, everything, blocks, 0)
+            (sent,) = spectra(before, [residue], None, everything, (blocks, 0))
             result = visibilities([[(exchange(sent), blocks, 0)]], result, [residue])
         return result.reshape(2, ch_dev, *result.shape[3:])
 
-    rest = blocks - 1
-    first, tail_first = spectra(None, [0, 2], 1, (0, 1), 1, 0)
+    (first,) = spectra(None, [0, 2], 1, everything, (blocks, 0))
     got_first = exchange(first)
-    second, tail_rest = spectra(None, [0, 2], 1, (1, blocks), rest, 0)
-    before = history(jnp.concatenate([tail_first, tail_rest], axis=0))
+    before = history(last_frames(voltages, filter_taps.shape[0] - 1, first))
+    size = 2 * blocks + blocks // 2
+    (second,) = spectra(before, [0, 2], 0, everything, (size, 0))
+    (second,) = spectra(before, [1], None, everything, (size, blocks, second))
+    second, third = spectra(before, [3], None, everything, (2 * size, 4 * blocks, second), (blocks, 0))
     got_second = exchange(second)
-    (third,) = spectra(before, [0, 2], 0, everything, 2 * blocks, 0)
-    (third,) = spectra(before, [1], None, everything, 2 * blocks, blocks, third)
     got_third = exchange(third)
-    (fourth,) = spectra(before, [3], None, everything, blocks, 0)
-    got_fourth = exchange(fourth)
-    late = [(got_first, 1, 0), (got_second, rest, 0)]
-    early = [(got_third, blocks, 0)]
-    result = visibilities([late, early], None, [0, 2])
-    result = visibilities([[(got_third, blocks, blocks)]], result, [1])
-    result = visibilities([[(got_fourth, blocks, 0)]], result, [3])
+    streams = [[(got_first, blocks, 0)], [(got_second, blocks, 0)]]
+    result = visibilities(streams, None, [0, 2])
+    result = visibilities([[(got_second, blocks, blocks)]], result, [1])
+    result = visibilities([[(got_second, blocks, 4 * blocks)]], result, [3], (0, GROUP // 2))
+    result = visibilities([[(got_third, blocks, 0)]], result, [3], (GROUP // 2, GROUP))
     return result.reshape(2, ch_dev, *result.shape[3:])
 
 

time: 415 us -> 405 us (0.976)
  blocking collectives: 0 us -> 234 us
  waiting for transfers between devices: 285 us -> 62.6 us
  starting transfers between devices: 25.5 us -> 13.7 us
  Pallas kernels: 101 us -> 93.6 us
    all_to_all x0 -> x1, blocking collectives: none -> 234 us  [exchange(): lax.all_to_all(payload, AXES, split_axis=0, concat_axis=0, tiled=True)]
    all_to_all x4 -> x2, waiting for transfers between devices: 283 us -> 60.6 us  [exchange(): lax.all_to_all(payload, AXES, split_axis=0, concat_axis=0, tiled=True)]
    pallas_call x5 -> x4, Pallas kernels: 70.7 us -> 58.8 us  [transform(): pl.pallas_call(functools.partial(transform_kernel, folds, tiles, has_base...]
    all_to_all x4 -> x2, starting transfers between devices: 23.4 us -> 11.6 us  [exchange(): lax.all_to_all(payload, AXES, split_axis=0, concat_axis=0, tiled=True)]
    pallas_call x3 -> x4, Pallas kernels: 30.5 us -> 32 us  [correlate(): pl.pallas_call(functools.partial(correlate_kernel, n_inp, n_tm, frames, p...]
  transfers between devices with their start and end apart: 5 -> 3, of which waited for: 5 -> 3; matrix products, arithmetic and copies ran while one was open for 0% -> 0% of each run, Pallas kernels for 21% -> 19%
where the time goes in v2:
time: 405 us
  blocking collectives  234 us (58%)
  Pallas kernels  93.6 us (23%)
  waiting for transfers between devices  62.6 us (15%)
  starting transfers between devices  13.7 us (3%)
    all_to_all x1, blocking collectives, exchange(): lax.all_to_all(payload, AXES, split_axis=0, concat_axis=0, tiled=True)  234 us
    all_to_all x2, waiting for transfers between devices, exchange(): lax.all_to_all(payload, AXES, split_axis=0, concat_axis=0, tiled=True)  60.6 us
    pallas_call x4, Pallas kernels, transform(): pl.pallas_call(functools.partial(transform_kernel, folds, tiles, has_base...  58.8 us
    pallas_call x4, Pallas kernels, correlate(): pl.pallas_call(functools.partial(correlate_kernel, n_inp, n_tm, frames, p...  32 us
    all_to_all x2, starting transfers between devices, exchange(): lax.all_to_all(payload, AXES, split_axis=0, concat_axis=0, tiled=True)  11.6 us
  transfers between devices with their start and end apart: 3, of which 3 were waited for; matrix products, arithmetic and copies ran while one was open for 0% of the time, Pallas kernels for 19%

profile of v2, /device:TPU:0, one launch (start us, length us, event | category | flops | bytes accessed | tf_op | source)
XLA Modules:
  0.0 404.7 jit_solution(6631356057265091358)
XLA Ops:
  0.0 12.0 %spectra_0_2_half1.1._ = f32[32,256,128]{2,1,0:T(8,128)} custom-call(f32[4,2048]{1,0:T(4,128)} %taps_ref.7, f32[32,64,2048]{2,1,0:T(8,128)} %rest_15_.7, f32[32,64,2048]{2,1,0:T(8,128)} %rest_15_.7, f32[32,64,2048]{2,1,0:T(8,128)} %rest_15_.7, f32[32,64,2048]{2,1,0:T(8,128)} %rest_15_.7, f32[32,64,2048]{2,1,0:T(8,128)} %rest_15_.7, ...), custom_call_target="tpu_custom_call" | custom-call | flops 3221225472 | bytes 8388608 | tf_op jit(solution)/shard_map/spectra_0_2_half1/pallas_call | solution.py:232
  12.0 7.4 %all-to-all-start.2 = ((f32[32,256,128]{2,1,0:T(8,128)}), f32[32,256,128]{2,1,0:T(8,128)}, u32[]{:S(2)}, u32[]{:S(2)}) async-start(f32[32,256,128]{2,1,0:T(8,128)} %spectra_0_2_half1.1._), calls=%async_computation.2 | async-start | bytes 8388608 | tf_op jit(solution)/shard_map/all_to_all | solution.py:348
  19.4 2.7 last_frames.1
  22.1 2.1 collective-permute-start
  24.2 2.1 collective-permute-done.before_ref
  26.3 0.0 copy-start
  26.3 0.9 copy-done
  27.1 12.1 %spectra_0_2_half0.1.rest_18_ = f32[32,640,128]{2,1,0:T(8,128)} custom-call(f32[4,2048]{1,0:T(4,128)} %taps_ref.7, f32[96,2048]{1,0:T(8,128)} %copy-done, f32[32,64,2048]{2,1,0:T(8,128)} %rest_15_.7, f32[32,64,2048]{2,1,0:T(8,128)} %rest_15_.7, f32[32,64,2048]{2,1,0:T(8,128)} %rest_15_.7, f32[32,64,2048]{2,1,0:T(8,128)} %rest_15_.7, ...), custom_call_target="tpu_custom_call" | custom-call | flops 3221225472 | bytes 8388608 | tf_op jit(solution)/shard_map/spectra_0_2_half0/pallas_call | solution.py:232
  39.3 17.3 %spectra_1.1.rest_18_ = f32[32,640,128]{2,1,0:T(8,128)} custom-call(f32[4,2048]{1,0:T(4,128)} %taps_ref.7, f32[96,2048]{1,0:T(8,128)} %copy-done, f32[32,64,2048]{2,1,0:T(8,128)} %rest_15_.7, f32[32,64,2048]{2,1,0:T(8,128)} %rest_15_.7, f32[32,64,2048]{2,1,0:T(8,128)} %rest_15_.7, f32[32,64,2048]{2,1,0:T(8,128)} %rest_15_.7, ...), custom_call_target="tpu_custom_call", output_to_operand_aliasing={{}: (20, {})} | custom-call | flops 6442450944 | bytes 16777216 | tf_op jit(solution)/shard_map/spectra_1/pallas_call | solution.py:232
  56.6 17.4 %spectra_3.1 = (f32[32,640,128]{2,1,0:T(8,128)}, f32[32,128,128]{2,1,0:T(8,128)}) custom-call(f32[4,2048]{1,0:T(4,128)} %taps_ref.7, f32[96,2048]{1,0:T(8,128)} %copy-done, f32[32,64,2048]{2,1,0:T(8,128)} %rest_15_.7, f32[32,64,2048]{2,1,0:T(8,128)} %rest_15_.7, f32[32,64,2048]{2,1,0:T(8,128)} %rest_15_.7, ...), custom_call_target="tpu_custom_call", output_to_operand_aliasing={{0}: (20, {})} | custom-call | flops 6442450944 | bytes 16777216 | tf_op jit(solution)/shard_map/spectra_3/pallas_call | solution.py:232
  74.0 39.7 %all-to-all-done.2 = f32[32,256,128]{2,1,0:T(8,128)} async-done(((f32[32,256,128]{2,1,0:T(8,128)}), f32[32,256,128]{2,1,0:T(8,128)}, u32[]{:S(2)}, u32[]{:S(2)}) %all-to-all-start.2) | async-done | bytes 4194336 | tf_op jit(solution)/shard_map/all_to_all | solution.py:348
  113.8 233.9 %all_to_all.15 = f32[32,640,128]{2,1,0:T(8,128)} all-to-all(f32[32,640,128]{2,1,0:T(8,128)} %get-tuple-element.8), channel_id=1, replica_groups=mesh['inp'=8,'tm'=4] {'inp','tm'}, dimensions={0} | all-to-all | bytes 20971520 | tf_op jit(solution)/shard_map/all_to_all | solution.py:348
  347.6 4.2 %all-to-all-start = ((f32[32,128,128]{2,1,0:T(8,128)}), f32[32,128,128]{2,1,0:T(8,128)}, u32[]{:S(2)}, u32[]{:S(2)}) async-start(f32[32,128,128]{2,1,0:T(8,128)} %get-tuple-element.7), calls=%async_computation | async-start | bytes 4194304 | tf_op jit(solution)/shard_map/all_to_all | solution.py:348
  351.8 16.3 %correlate_0_2_from0.1.rest_1_ = f32[2,8,4,256,256]{4,3,2,1,0:T(8,128)} custom-call(f32[32,4,64,128]{3,2,1,0:T(8,128)} %bitcast.3.rest_0_, f32[32,10,64,128]{3,2,1,0:T(8,128)} %bitcast.5), custom_call_target="tpu_custom_call" | custom-call | flops 6442450944 | bytes 16777216 | tf_op jit(solution)/shard_map/correlate_0_2_from0/pallas_call | solution.py:316
  368.2 7.1 %correlate_1_from0.1.rest_1_ = f32[2,8,4,256,256]{4,3,2,1,0:T(8,128)} custom-call(f32[32,10,64,128]{3,2,1,0:T(8,128)} %bitcast.6, f32[2,8,4,256,256]{4,3,2,1,0:T(8,128)} %correlate_0_2_from0.1.rest_1_), custom_call_target="tpu_custom_call", output_to_operand_aliasing={{}: (1, {})} | custom-call | flops 3221225472 | bytes 8388608 | tf_op jit(solution)/shard_map/correlate_1_from0/pallas_call | solution.py:316
  375.2 4.3 %correlate_3_from0.1.rest_1_ = f32[2,8,4,256,256]{4,3,2,1,0:T(8,128)} custom-call(f32[32,20,32,128]{3,2,1,0:T(8,128)} %bitcast.7, f32[2,8,4,256,256]{4,3,2,1,0:T(8,128)} %correlate_1_from0.1.rest_1_), custom_call_target="tpu_custom_call", output_to_operand_aliasing={{}: (1, {})} | custom-call | flops 1610612736 | bytes 4194304 | tf_op jit(solution)/shard_map/correlate_3_from0/pallas_call | solution.py:316
  379.6 20.8 %all-to-all-done = f32[32,128,128]{2,1,0:T(8,128)} async-done(((f32[32,128,128]{2,1,0:T(8,128)}), f32[32,128,128]{2,1,0:T(8,128)}, u32[]{:S(2)}, u32[]{:S(2)}) %all-to-all-start) | async-done | bytes 2097184 | tf_op jit(solution)/shard_map/all_to_all | solution.py:348
  400.4 4.3 %correlate_3_from4.1 = f32[2,8,4,256,256]{4,3,2,1,0:T(8,128)} custom-call(f32[32,4,32,128]{3,2,1,0:T(8,128)} %bitcast.rest_0_, f32[2,8,4,256,256]{4,3,2,1,0:T(8,128)} %correlate_3_from0.1.rest_1_), custom_call_target="tpu_custom_call", output_to_operand_aliasing={{}: (1, {})} | custom-call | flops 1610612736 | bytes 4194304 | tf_op jit(solution)/shard_map/correlate_3_from4/pallas_call | solution.py:316
Async XLA Ops:
  12.0 101.8 %all-to-all-start.2 = ((f32[32,256,128]{2,1,0:T(8,128)}), f32[32,256,128]{2,1,0:T(8,128)}, u32[]{:S(2)}, u32[]{:S(2)}) async-start(f32[32,256,128]{2,1,0:T(8,128)} %spectra_0_2_half1.1._), calls=%async_computation.2 | async-start | bytes 8388608 | tf_op jit(solution)/shard_map/all_to_all | solution.py:348
  22.1 4.2 %collective-permute-start = (f32[96,2048]{1,0:T(8,128)}, f32[96,2048]{1,0:T(8,128)S(1)}, u32[]{:S(2)}, u32[]{:S(2)}) collective-permute-start(f32[96,2048]{1,0:T(8,128)} %last_frames.1), channel_id=1, source_target_pairs={{0,1},{1,2},{2,3},{4,5},{5,6},{6,7},{8,9},{9,10},{10,11},{12,13},{... | collective-permute-start | bytes 2359304 | tf_op jit(solution)/shard_map/ppermute | solution.py:345
  26.3 0.9 copy-start
  347.6 52.8 %all-to-all-start = ((f32[32,128,128]{2,1,0:T(8,128)}), f32[32,128,128]{2,1,0:T(8,128)}, u32[]{:S(2)}, u32[]{:S(2)}) async-start(f32[32,128,128]{2,1,0:T(8,128)} %get-tuple-element.7), calls=%async_computation | async-start | bytes 4194304 | tf_op jit(solution)/shard_map/all_to_all | solution.py:348

commit v3 on v2

--- a/solution.py
+++ b/solution.py
@@ -281,11 +281,12 @@
                 turned = jnp.where(
                     first, pltpu.roll(value, LANES - width, 1), -pltpu.roll(value, width, 1)
                 )
-            columns.append(split(value) + split(turned))
-        p_hi, p_lo, t_hi, t_lo = [jnp.concatenate(column, axis=1) for column in zip(*columns)]
-        right = jnp.concatenate([p_hi, p_hi, p_lo], axis=1)
-        out[0, c, 0] = dot_nt(jnp.concatenate([p_hi, p_lo, p_hi], axis=1), right) * scale
-        out[1, c, 0] = dot_nt(jnp.concatenate([t_hi, t_lo, t_hi], axis=1), right) * scale
+            columns.append(split(value) + (turned.astype(jnp.bfloat16),))
+        p_hi, p_lo, t_hi = [jnp.concatenate(column, axis=1) for column in zip(*columns)]
+        plain = dot_nt(p_hi, p_lo)
+        twist = dot_nt(t_hi, p_lo)
+        out[0, c, 0] = (dot_nt(p_hi, p_hi) + (plain + plain.T)) * scale
+        out[1, c, 0] = (dot_nt(t_hi, p_hi) + (twist - twist.T)) * scale
 
 
 def correlate(streams, base, n_inp, n_tm, inputs_dev, frames, ch_dev, step, residues, channels):

time: 405 us -> 405 us (level)
  no operation moved by 1% of the time
where the time goes in v3:
time: 405 us; the launch traced here: 404 us
  blocking collectives  234 us (58%)
  Pallas kernels  92.1 us (23%)
  waiting for transfers between devices  63.5 us (16%)
  starting transfers between devices  13.7 us (3%)
    all_to_all x1, blocking collectives, exchange(): lax.all_to_all(payload, AXES, split_axis=0, concat_axis=0, tiled=True)  234 us
    all_to_all x2, waiting for transfers between devices, exchange(): lax.all_to_all(payload, AXES, split_axis=0, concat_axis=0, tiled=True)  61.4 us
    pallas_call x4, Pallas kernels, transform(): pl.pallas_call(functools.partial(transform_kernel, folds, tiles, has_base...  58.8 us
    pallas_call x4, Pallas kernels, correlate(): pl.pallas_call(functools.partial(correlate_kernel, n_inp, n_tm, frames, p...  30.6 us
    all_to_all x2, starting transfers between devices, exchange(): lax.all_to_all(payload, AXES, split_axis=0, concat_axis=0, tiled=True)  11.6 us
  transfers between devices with their start and end apart: 3, of which 3 were waited for; matrix products, arithmetic and copies ran while one was open for 0% of the time, Pallas kernels for 19%

profile of v3, /device:TPU:0, one launch (start us, length us, event | category | flops | bytes accessed | tf_op | source)
XLA Modules:
  0.0 404.2 jit_solution(12477979318296750967)
XLA Ops:
  0.0 12.0 %spectra_0_2_half1.1._ = f32[32,256,128]{2,1,0:T(8,128)} custom-call(f32[4,2048]{1,0:T(4,128)} %taps_ref.7, f32[32,64,2048]{2,1,0:T(8,128)} %rest_15_.7, f32[32,64,2048]{2,1,0:T(8,128)} %rest_15_.7, f32[32,64,2048]{2,1,0:T(8,128)} %rest_15_.7, f32[32,64,2048]{2,1,0:T(8,128)} %rest_15_.7, f32[32,64,2048]{2,1,0:T(8,128)} %rest_15_.7, ...), custom_call_target="tpu_custom_call" | custom-call | flops 3221225472 | bytes 8388608 | tf_op jit(solution)/shard_map/spectra_0_2_half1/pallas_call | solution.py:232
  12.0 7.4 %all-to-all-start.2 = ((f32[32,256,128]{2,1,0:T(8,128)}), f32[32,256,128]{2,1,0:T(8,128)}, u32[]{:S(2)}, u32[]{:S(2)}) async-start(f32[32,256,128]{2,1,0:T(8,128)} %spectra_0_2_half1.1._), calls=%async_computation.2 | async-start | bytes 8388608 | tf_op jit(solution)/shard_map/all_to_all | solution.py:349
  19.4 2.7 last_frames.1
  22.1 2.1 collective-permute-start
  24.2 2.1 collective-permute-done.before_ref
  26.3 0.0 copy-start
  26.3 0.9 copy-done
  27.1 12.1 %spectra_0_2_half0.1.rest_18_ = f32[32,640,128]{2,1,0:T(8,128)} custom-call(f32[4,2048]{1,0:T(4,128)} %taps_ref.7, f32[96,2048]{1,0:T(8,128)} %copy-done, f32[32,64,2048]{2,1,0:T(8,128)} %rest_15_.7, f32[32,64,2048]{2,1,0:T(8,128)} %rest_15_.7, f32[32,64,2048]{2,1,0:T(8,128)} %rest_15_.7, f32[32,64,2048]{2,1,0:T(8,128)} %rest_15_.7, ...), custom_call_target="tpu_custom_call" | custom-call | flops 3221225472 | bytes 8388608 | tf_op jit(solution)/shard_map/spectra_0_2_half0/pallas_call | solution.py:232
  39.3 17.3 %spectra_1.1.rest_18_ = f32[32,640,128]{2,1,0:T(8,128)} custom-call(f32[4,2048]{1,0:T(4,128)} %taps_ref.7, f32[96,2048]{1,0:T(8,128)} %copy-done, f32[32,64,2048]{2,1,0:T(8,128)} %rest_15_.7, f32[32,64,2048]{2,1,0:T(8,128)} %rest_15_.7, f32[32,64,2048]{2,1,0:T(8,128)} %rest_15_.7, f32[32,64,2048]{2,1,0:T(8,128)} %rest_15_.7, ...), custom_call_target="tpu_custom_call", output_to_operand_aliasing={{}: (20, {})} | custom-call | flops 6442450944 | bytes 16777216 | tf_op jit(solution)/shard_map/spectra_1/pallas_call | solution.py:232
  56.6 17.4 %spectra_3.1 = (f32[32,640,128]{2,1,0:T(8,128)}, f32[32,128,128]{2,1,0:T(8,128)}) custom-call(f32[4,2048]{1,0:T(4,128)} %taps_ref.7, f32[96,2048]{1,0:T(8,128)} %copy-done, f32[32,64,2048]{2,1,0:T(8,128)} %rest_15_.7, f32[32,64,2048]{2,1,0:T(8,128)} %rest_15_.7, f32[32,64,2048]{2,1,0:T(8,128)} %rest_15_.7, ...), custom_call_target="tpu_custom_call", output_to_operand_aliasing={{0}: (20, {})} | custom-call | flops 6442450944 | bytes 16777216 | tf_op jit(solution)/shard_map/spectra_3/pallas_call | solution.py:232
  74.0 39.7 %all-to-all-done.2 = f32[32,256,128]{2,1,0:T(8,128)} async-done(((f32[32,256,128]{2,1,0:T(8,128)}), f32[32,256,128]{2,1,0:T(8,128)}, u32[]{:S(2)}, u32[]{:S(2)}) %all-to-all-start.2) | async-done | bytes 4194336 | tf_op jit(solution)/shard_map/all_to_all | solution.py:349
  113.8 233.9 %all_to_all.15 = f32[32,640,128]{2,1,0:T(8,128)} all-to-all(f32[32,640,128]{2,1,0:T(8,128)} %get-tuple-element.8), channel_id=1, replica_groups=mesh['inp'=8,'tm'=4] {'inp','tm'}, dimensions={0} | all-to-all | bytes 20971520 | tf_op jit(solution)/shard_map/all_to_all | solution.py:349
  347.6 4.2 %all-to-all-start = ((f32[32,128,128]{2,1,0:T(8,128)}), f32[32,128,128]{2,1,0:T(8,128)}, u32[]{:S(2)}, u32[]{:S(2)}) async-start(f32[32,128,128]{2,1,0:T(8,128)} %get-tuple-element.7), calls=%async_computation | async-start | bytes 4194304 | tf_op jit(solution)/shard_map/all_to_all | solution.py:349
  351.8 16.9 %correlate_0_2_from0.1.rest_1_ = f32[2,8,4,256,256]{4,3,2,1,0:T(8,128)} custom-call(f32[32,4,64,128]{3,2,1,0:T(8,128)} %bitcast.3.rest_0_, f32[32,10,64,128]{3,2,1,0:T(8,128)} %bitcast.5), custom_call_target="tpu_custom_call" | custom-call | flops 6442450944 | bytes 16777216 | tf_op jit(solution)/shard_map/correlate_0_2_from0/pallas_call | solution.py:317
  368.7 6.2 %correlate_1_from0.1.rest_1_ = f32[2,8,4,256,256]{4,3,2,1,0:T(8,128)} custom-call(f32[32,10,64,128]{3,2,1,0:T(8,128)} %bitcast.6, f32[2,8,4,256,256]{4,3,2,1,0:T(8,128)} %correlate_0_2_from0.1.rest_1_), custom_call_target="tpu_custom_call", output_to_operand_aliasing={{}: (1, {})} | custom-call | flops 3221225472 | bytes 8388608 | tf_op jit(solution)/shard_map/correlate_1_from0/pallas_call | solution.py:317
  374.9 3.8 correlate_3_from0.1.rest_1_
  378.7 21.7 %all-to-all-done = f32[32,128,128]{2,1,0:T(8,128)} async-done(((f32[32,128,128]{2,1,0:T(8,128)}), f32[32,128,128]{2,1,0:T(8,128)}, u32[]{:S(2)}, u32[]{:S(2)}) %all-to-all-start) | async-done | bytes 2097184 | tf_op jit(solution)/shard_map/all_to_all | solution.py:349
  400.4 3.8 correlate_3_from4.1
Async XLA Ops:
  12.0 101.8 %all-to-all-start.2 = ((f32[32,256,128]{2,1,0:T(8,128)}), f32[32,256,128]{2,1,0:T(8,128)}, u32[]{:S(2)}, u32[]{:S(2)}) async-start(f32[32,256,128]{2,1,0:T(8,128)} %spectra_0_2_half1.1._), calls=%async_computation.2 | async-start | bytes 8388608 | tf_op jit(solution)/shard_map/all_to_all | solution.py:349
  22.1 4.2 %collective-permute-start = (f32[96,2048]{1,0:T(8,128)}, f32[96,2048]{1,0:T(8,128)S(1)}, u32[]{:S(2)}, u32[]{:S(2)}) collective-permute-start(f32[96,2048]{1,0:T(8,128)} %last_frames.1), channel_id=1, source_target_pairs={{0,1},{1,2},{2,3},{4,5},{5,6},{6,7},{8,9},{9,10},{10,11},{12,13},{... | collective-permute-start | bytes 2359304 | tf_op jit(solution)/shard_map/ppermute | solution.py:346
  26.3 0.9 copy-start
  347.6 52.8 %all-to-all-start = ((f32[32,128,128]{2,1,0:T(8,128)}), f32[32,128,128]{2,1,0:T(8,128)}, u32[]{:S(2)}, u32[]{:S(2)}) async-start(f32[32,128,128]{2,1,0:T(8,128)} %get-tuple-element.7), calls=%async_computation | async-start | bytes 4194304 | tf_op jit(solution)/shard_map/all_to_all | solution.py:349

commit v4 on v2

--- a/solution.py
+++ b/solution.py
@@ -239,7 +239,7 @@
             pl.BlockSpec((count, share, LANES), lambda b, at=place[1]: (0, b + at, 0)) for place in places
         ],
         scratch_shapes=scratch,
-        compiler_params=pltpu.CompilerParams(vmem_limit_bytes=VMEM_BYTES),
+        compiler_params=pltpu.CompilerParams(vmem_limit_bytes=VMEM_BYTES if half is None else 24 * 1024 * 1024),
         cost_estimate=pl.CostEstimate(
             flops=flops, bytes_accessed=4 * blocks * BLOCK * frames * nfft, transcendentals=0
         ),

time: 405 us -> 421 us (1.040)
  local copies, waits for them, and re-layouts: 0.88 us -> 22.5 us
  waiting for transfers between devices: 62.6 us -> 55.7 us
    unnamed x2 -> x30, local copies, waits for them, and re-layouts: 0.88 us -> 22.5 us
    all_to_all x2, waiting for transfers between devices: 60.6 us -> 53.7 us  [exchange(): lax.all_to_all(payload, AXES, split_axis=0, concat_axis=0, tiled=True)]
    all_to_all x1, blocking collectives: 234 us -> 238 us  [exchange(): lax.all_to_all(payload, AXES, split_axis=0, concat_axis=0, tiled=True)]
  transfers between devices with their start and end apart: 3 -> 3, of which waited for: 3 -> 3; matrix products, arithmetic and copies ran while one was open for 0% -> 0% of each run, Pallas kernels for 19% -> 18%
where the time goes in v4:
time: 421 us; the launch traced here: 420 us
  blocking collectives  238 us (57%)
  Pallas kernels  89.6 us (21%)
  waiting for transfers between devices  55.7 us (13%)
  local copies, waits for them, and re-layouts  22.5 us (5%)
  starting transfers between devices  13.6 us (3%)
    all_to_all x1, blocking collectives, exchange(): lax.all_to_all(payload, AXES, split_axis=0, concat_axis=0, tiled=True)  238 us
    pallas_call x4, Pallas kernels, transform(): pl.pallas_call(functools.partial(transform_kernel, folds, tiles, has_base...  54.8 us
    all_to_all x2, waiting for transfers between devices, exchange(): lax.all_to_all(payload, AXES, split_axis=0, concat_axis=0, tiled=True)  53.7 us
    pallas_call x4, Pallas kernels, correlate(): pl.pallas_call(functools.partial(correlate_kernel, n_inp, n_tm, frames, p...  32 us
    unnamed x30, local copies, waits for them, and re-layouts  22.5 us
    all_to_all x2, starting transfers between devices, exchange(): lax.all_to_all(payload, AXES, split_axis=0, concat_axis=0, tiled=True)  11.4 us
  transfers between devices with their start and end apart: 3, of which 3 were waited for; matrix products, arithmetic and copies ran while one was open for 0% of the time, Pallas kernels for 18%

profile of v4, /device:TPU:0, one launch (start us, length us, event | category | flops | bytes accessed | tf_op | source)
XLA Modules:
  0.0 419.7 jit_solution(3736868219147964585)
XLA Ops:
  0.0 5.8 %copy-done = f32[32,64,2048]{2,1,0:T(8,128)S(1)} copy-done((f32[32,64,2048]{2,1,0:T(8,128)S(1)}, f32[32,64,2048]{2,1,0:T(8,128)}, u32[]{:S(2)}) %copy-start) | copy-done | bytes 16777240
  5.8 1.0 copy-done.5
  6.8 1.0 copy-done.7
  7.9 1.0 copy-done.9
  8.9 1.0 copy-done.11
  10.7 10.0 %spectra_0_2_half1.1._ = f32[32,256,128]{2,1,0:T(8,128)S(1)} custom-call(f32[4,2048]{1,0:T(4,128)S(1)} %copy-done.13, f32[32,64,2048]{2,1,0:T(8,128)S(1)} %copy-done, f32[32,64,2048]{2,1,0:T(8,128)S(1)} %copy-done, f32[32,64,2048]{2,1,0:T(8,128)S(1)} %copy-done, f32[32,64,2048]{2,1,0:T(8,128)S(1)} %copy-done, f32[32,64,2048]{2,1,0:T(8,128)S(1)} %copy-done, ...), custom_call_target="tpu_custom_call" | custom-call | flops 3221225472 | bytes 8388608 | tf_op jit(solution)/shard_map/spectra_0_2_half1/pallas_call | solution.py:232
  20.8 1.9 copy-done.3
  22.7 7.4 %all-to-all-start.2 = ((f32[32,256,128]{2,1,0:T(8,128)}), f32[32,256,128]{2,1,0:T(8,128)}, u32[]{:S(2)}, u32[]{:S(2)}) async-start(f32[32,256,128]{2,1,0:T(8,128)} %copy-done.3), calls=%async_computation.2 | async-start | bytes 8388608 | tf_op jit(solution)/shard_map/all_to_all | solution.py:348
  30.2 2.8 last_frames.1
  33.0 2.1 collective-permute-start
  35.1 2.1 collective-permute-done.before_ref
  37.2 5.8 %copy-done.1 = f32[32,64,2048]{2,1,0:T(8,128)S(1)} copy-done((f32[32,64,2048]{2,1,0:T(8,128)S(1)}, f32[32,64,2048]{2,1,0:T(8,128)}, u32[]{:S(2)}) %copy-start.1) | copy-done | bytes 16777240
  43.0 10.0 %spectra_0_2_half0.1.rest_18_ = f32[32,640,128]{2,1,0:T(8,128)S(1)} custom-call(f32[4,2048]{1,0:T(4,128)S(1)} %copy-done.14, f32[96,2048]{1,0:T(8,128)S(1)} %collective-permute-done.before_ref, f32[32,64,2048]{2,1,0:T(8,128)S(1)} %copy-done.1, f32[32,64,2048]{2,1,0:T(8,128)S(1)} %copy-done.1, f32[32,64,2048]{2,1,0:T(8,128)S(1)} %copy-done.1, ...), custom_call_target="tpu_custom_call" | custom-call | flops 3221225472 | bytes 8388608 | tf_op jit(solution)/shard_map/spectra_0_2_half0/pallas_call | solution.py:232
  53.0 4.1 copy-done.2
  57.1 17.3 %spectra_1.1.rest_18_ = f32[32,640,128]{2,1,0:T(8,128)} custom-call(f32[4,2048]{1,0:T(4,128)} %taps_ref.7, f32[96,2048]{1,0:T(8,128)} %copy-done.4, f32[32,64,2048]{2,1,0:T(8,128)} %rest_15_.7, f32[32,64,2048]{2,1,0:T(8,128)} %rest_15_.7, f32[32,64,2048]{2,1,0:T(8,128)} %rest_15_.7, f32[32,64,2048]{2,1,0:T(8,128)} %rest_15_.7, ...), custom_call_target="tpu_custom_call", output_to_operand_aliasing={{}: (20, {})} | custom-call | flops 6442450944 | bytes 16777216 | tf_op jit(solution)/shard_map/spectra_1/pallas_call | solution.py:232
  74.4 17.4 %spectra_3.1 = (f32[32,640,128]{2,1,0:T(8,128)}, f32[32,128,128]{2,1,0:T(8,128)}) custom-call(f32[4,2048]{1,0:T(4,128)} %taps_ref.7, f32[96,2048]{1,0:T(8,128)} %copy-done.4, f32[32,64,2048]{2,1,0:T(8,128)} %rest_15_.7, f32[32,64,2048]{2,1,0:T(8,128)} %rest_15_.7, f32[32,64,2048]{2,1,0:T(8,128)} %rest_15_.7, ...), custom_call_target="tpu_custom_call", output_to_operand_aliasing={{0}: (20, {})} | custom-call | flops 6442450944 | bytes 16777216 | tf_op jit(solution)/shard_map/spectra_3/pallas_call | solution.py:232
  91.9 32.6 %all-to-all-done.2 = f32[32,256,128]{2,1,0:T(8,128)} async-done(((f32[32,256,128]{2,1,0:T(8,128)}), f32[32,256,128]{2,1,0:T(8,128)}, u32[]{:S(2)}, u32[]{:S(2)}) %all-to-all-start.2) | async-done | bytes 4194336 | tf_op jit(solution)/shard_map/all_to_all | solution.py:348
  124.5 238.1 %all_to_all.15 = f32[32,640,128]{2,1,0:T(8,128)} all-to-all(f32[32,640,128]{2,1,0:T(8,128)} %get-tuple-element.8), channel_id=1, replica_groups=mesh['inp'=8,'tm'=4] {'inp','tm'}, dimensions={0} | all-to-all | bytes 20971520 | tf_op jit(solution)/shard_map/all_to_all | solution.py:348
  362.6 4.0 all-to-all-start
  366.6 16.3 %correlate_0_2_from0.1.rest_1_ = f32[2,8,4,256,256]{4,3,2,1,0:T(8,128)} custom-call(f32[32,4,64,128]{3,2,1,0:T(8,128)} %bitcast.3.rest_0_, f32[32,10,64,128]{3,2,1,0:T(8,128)} %bitcast.5), custom_call_target="tpu_custom_call" | custom-call | flops 6442450944 | bytes 16777216 | tf_op jit(solution)/shard_map/correlate_0_2_from0/pallas_call | solution.py:316
  383.0 7.1 %correlate_1_from0.1.rest_1_ = f32[2,8,4,256,256]{4,3,2,1,0:T(8,128)} custom-call(f32[32,10,64,128]{3,2,1,0:T(8,128)} %bitcast.6, f32[2,8,4,256,256]{4,3,2,1,0:T(8,128)} %correlate_0_2_from0.1.rest_1_), custom_call_target="tpu_custom_call", output_to_operand_aliasing={{}: (1, {})} | custom-call | flops 3221225472 | bytes 8388608 | tf_op jit(solution)/shard_map/correlate_1_from0/pallas_call | solution.py:316
  390.0 4.3 %correlate_3_from0.1.rest_1_ = f32[2,8,4,256,256]{4,3,2,1,0:T(8,128)} custom-call(f32[32,20,32,128]{3,2,1,0:T(8,128)} %bitcast.7, f32[2,8,4,256,256]{4,3,2,1,0:T(8,128)} %correlate_1_from0.1.rest_1_), custom_call_target="tpu_custom_call", output_to_operand_aliasing={{}: (1, {})} | custom-call | flops 1610612736 | bytes 4194304 | tf_op jit(solution)/shard_map/correlate_3_from0/pallas_call | solution.py:316
  394.4 21.0 %all-to-all-done = f32[32,128,128]{2,1,0:T(8,128)} async-done(((f32[32,128,128]{2,1,0:T(8,128)}), f32[32,128,128]{2,1,0:T(8,128)}, u32[]{:S(2)}, u32[]{:S(2)}) %all-to-all-start) | async-done | bytes 2097184 | tf_op jit(solution)/shard_map/all_to_all | solution.py:348
  415.4 4.3 %correlate_3_from4.1 = f32[2,8,4,256,256]{4,3,2,1,0:T(8,128)} custom-call(f32[32,4,32,128]{3,2,1,0:T(8,128)} %bitcast.rest_0_, f32[2,8,4,256,256]{4,3,2,1,0:T(8,128)} %correlate_3_from0.1.rest_1_), custom_call_target="tpu_custom_call", output_to_operand_aliasing={{}: (1, {})} | custom-call | flops 1610612736 | bytes 4194304 | tf_op jit(solution)/shard_map/correlate_3_from4/pallas_call | solution.py:316
  (22 shorter events, 0.8 us)
Async XLA Ops:
  0.0 5.8 %copy-start = (f32[32,64,2048]{2,1,0:T(8,128)S(1)}, f32[32,64,2048]{2,1,0:T(8,128)}, u32[]{:S(2)}) copy-start(f32[32,64,2048]{2,1,0:T(8,128)} %rest_15_.7) | copy-start | bytes 50331652
  5.8 1.0 copy-start.5
  6.8 1.0 copy-start.7
  7.9 1.0 copy-start.9
  8.9 1.0 copy-start.11
  9.9 0.8 copy-start.13
  20.8 1.9 copy-start.3
  22.7 101.8 %all-to-all-start.2 = ((f32[32,256,128]{2,1,0:T(8,128)}), f32[32,256,128]{2,1,0:T(8,128)}, u32[]{:S(2)}, u32[]{:S(2)}) async-start(f32[32,256,128]{2,1,0:T(8,128)} %copy-done.3), calls=%async_computation.2 | async-start | bytes 8388608 | tf_op jit(solution)/shard_map/all_to_all | solution.py:348
  30.1 7.1 %copy-start.6 = (bf16[512,512]{1,0:T(8,128)(2,1)S(1)}, bf16[512,512]{1,0:T(8,128)(2,1)}, u32[]{:S(2)}) copy-start(bf16[512,512]{1,0:T(8,128)(2,1)} %constant.19.clone.rest_19_) | copy-start | bytes 1572868
  30.2 7.1 %copy-start.8 = (bf16[512,512]{1,0:T(8,128)(2,1)S(1)}, bf16[512,512]{1,0:T(8,128)(2,1)}, u32[]{:S(2)}) copy-start(bf16[512,512]{1,0:T(8,128)(2,1)} %constant.18.clone.rest_18_) | copy-start | bytes 1572868
  30.2 7.0 %copy-start.10 = (bf16[512,512]{1,0:T(8,128)(2,1)S(1)}, bf16[512,512]{1,0:T(8,128)(2,1)}, u32[]{:S(2)}) copy-start(bf16[512,512]{1,0:T(8,128)(2,1)} %constant.17.clone.rest_17_) | copy-start | bytes 1572868
  30.2 7.0 %copy-start.12 = (bf16[512,512]{1,0:T(8,128)(2,1)S(1)}, bf16[512,512]{1,0:T(8,128)(2,1)}, u32[]{:S(2)}) copy-start(bf16[512,512]{1,0:T(8,128)(2,1)} %constant.16.clone.rest_16_) | copy-start | bytes 1572868
  30.2 7.0 %copy-start.14 = (f32[4,2048]{1,0:T(4,128)S(1)}, f32[4,2048]{1,0:T(4,128)}, u32[]{:S(2)}) copy-start(f32[4,2048]{1,0:T(4,128)} %taps_ref.7) | copy-start | bytes 98308
  33.0 4.2 collective-permute-start
  37.2 5.8 %copy-start.1 = (f32[32,64,2048]{2,1,0:T(8,128)S(1)}, f32[32,64,2048]{2,1,0:T(8,128)}, u32[]{:S(2)}) copy-start(f32[32,64,2048]{2,1,0:T(8,128)} %rest_15_.7) | copy-start | bytes 50331652
  43.0 10.0 %copy-start.4 = (f32[96,2048]{1,0:T(8,128)}, f32[96,2048]{1,0:T(8,128)S(1)}, u32[]{:S(2)}) copy-start(f32[96,2048]{1,0:T(8,128)S(1)} %collective-permute-done.before_ref) | copy-start | bytes 2359300
  53.0 4.1 copy-start.2
  362.6 52.8 %all-to-all-start = ((f32[32,128,128]{2,1,0:T(8,128)}), f32[32,128,128]{2,1,0:T(8,128)}, u32[]{:S(2)}, u32[]{:S(2)}) async-start(f32[32,128,128]{2,1,0:T(8,128)} %get-tuple-element.7), calls=%async_computation | async-start | bytes 4194304 | tf_op jit(solution)/shard_map/all_to_all | solution.py:348
